TPU v7x, 32 devices: a whole 2x2x4 slice. The times are simulated.
32 devices in a mesh: groups: 2 (over y), dp: 4 (over z), mp: 2 (over x), pair: 2 (over core).
Axes of the slice: x: 2, y: 2, z: 4, core: 2. Of those that a mesh axis runs over, the one named last changes fastest.
Arguments:
- image_features: bfloat16 [2048, 1152], P(('groups', 'dp')), parts along dimension 0, may hold values from -6 to 6
- text_features: bfloat16 [2048, 1152], P(('groups', 'dp')), parts along dimension 0, may hold values from -6 to 6
- image_head: bfloat16 [1152, 1152], P(None, ('mp', 'pair')), may hold values from -0.0048828125 to 0.0048828125
- text_head: bfloat16 [1152, 1152], P(None, ('mp', 'pair')), may hold values from -0.0048828125 to 0.0048828125
- log_scale: float32 [1], replicated, may hold values from 1.6 to 2.6
- bias: float32 [1], replicated, may hold values from -3 to -1
Outputs:
- row_loss: float32 [2048], P(('groups', 'dp')), parts along dimension 0
- image_head_grad: float32 [2304, 1152], P(('groups', 'dp'), ('mp', 'pair')), parts along dimension 0
- text_head_grad: float32 [2304, 1152], P(('groups', 'dp'), ('mp', 'pair')), parts along dimension 0
There are 2 independent parts, one for each index of `groups`. A program takes and returns all parts, laid end to end along the dimension named above; an argument that names none is the same for every part. Nothing has to cross between parts.
All inputs are finite; a program needn't handle non-finite values.
Results may differ from a plain program's by a relative error of at most 0.0049.
Values may be sent and summed in bfloat16 or wider, within the bound.
A program may use at most 64 MiB of HBM per device.

v0:
```python
import jax
import jax.numpy as jnp
from jax import lax
from jax.sharding import PartitionSpec as P

epsilon = 1e-06


def from_behind(block, axis, distance):
    devices = range(lax.axis_size(axis))
    route = [((i - distance) % len(devices), i) for i in devices]
    return lax.ppermute(block, axis, route)


def backward(unit_rows, norm_rows, gradient, inner):
    return ((gradient - unit_rows * inner[:, None]) / norm_rows).astype(jnp.bfloat16)


def move_block(visiting):
    return from_behind(visiting, "dp", 1)


def body(image_features, text_features, image_head, text_head, log_scale, bias):
    block_rows = image_features.shape[0]
    cycle_size = lax.axis_size("dp")
    shards = lax.axis_size(("mp", "pair"))
    slice_rows = block_rows // shards
    proj_image = jnp.dot(image_features, image_head, preferred_element_type=jnp.float32)
    proj_text = jnp.dot(text_features, text_head, preferred_element_type=jnp.float32)
    square_image, square_text = lax.psum(
        (jnp.sum(proj_image * proj_image, axis=1), jnp.sum(proj_text * proj_text, axis=1)),
        ("mp", "pair"),
    )
    norm_image = jnp.sqrt(square_image + epsilon)[:, None]
    norm_text = jnp.sqrt(square_text + epsilon)[:, None]
    unit_image = proj_image / norm_image
    unit_text = proj_text / norm_text
    emb_image = unit_image.astype(jnp.bfloat16)
    emb_text = unit_text.astype(jnp.bfloat16)
    full_image = lax.all_gather(emb_image, ("mp", "pair"), axis=1, tiled=True)
    own_text = lax.all_to_all(emb_text, ("mp", "pair"), split_axis=0, concat_axis=1, tiled=True)
    full_width = full_image.shape[1]
    position = lax.axis_index(("mp", "pair"))
    my_block = lax.axis_index("dp")
    scale = jnp.exp(log_scale[0])
    offset = bias[0]
    row_ids = lax.broadcasted_iota(jnp.int32, (block_rows, slice_rows), 0)
    col_ids = lax.broadcasted_iota(jnp.int32, (block_rows, slice_rows), 1) + position * slice_rows
    diagonal = row_ids == col_ids
    zero_index = jnp.int32(0)

    def compare(turn, visiting, grad_image, loss_sum):
        partial_dots = lax.dot_general(
            full_image, visiting, (((1,), (1,)), ((), ())), preferred_element_type=jnp.float32
        )
        logits = scale * partial_dots + offset
        signs = jnp.where(diagonal & (turn == 0), jnp.float32(1.0), jnp.float32(-1.0))
        loss_sum = loss_sum + jnp.sum(jax.nn.softplus(-signs * logits), axis=1)
        weights = (-signs * jax.nn.sigmoid(-signs * logits) * (scale / block_rows)).astype(
            jnp.bfloat16
        )
        grad_image = grad_image + jnp.dot(weights, visiting, preferred_element_type=jnp.float32)
        update = lax.dot_general(
            weights, full_image, (((0,), (0,)), ((), ())), preferred_element_type=jnp.float32
        )
        return (grad_image, loss_sum, update)

    zero_grad = jnp.zeros((block_rows, full_width), jnp.float32)
    zero_loss = jnp.zeros((block_rows,), jnp.float32)
    store = jnp.zeros((cycle_size, slice_rows, full_width), jnp.float32)

    def advance_one(turn, state):
        visiting, text_grad, kept, grad_image, loss_sum = state
        grad_image, loss_sum, update = compare(turn, visiting, grad_image, loss_sum)
        source = (my_block - turn) % cycle_size
        kept = lax.dynamic_update_slice(kept, update[None], (source, zero_index, zero_index))
        visiting = move_block(visiting)
        return (visiting, text_grad, kept, grad_image, loss_sum)

    final = lax.fori_loop(0, cycle_size, advance_one, (own_text, None, store, zero_grad, zero_loss))
    store = final[2]
    grad_image = final[3]
    loss_sum = final[4]
    home_terms = lax.all_to_all(store, "dp", split_axis=0, concat_axis=0, tiled=True)
    grad_text_home = jnp.sum(home_terms, axis=0)
    grad_image_share = lax.psum_scatter(grad_image, ("mp", "pair"), scatter_dimension=1, tiled=True)
    grad_text_share = lax.all_to_all(
        grad_text_home, ("mp", "pair"), split_axis=1, concat_axis=0, tiled=True
    )
    inner_image, inner_text, loss_total = lax.psum(
        (
            jnp.sum(unit_image * grad_image_share, axis=1),
            jnp.sum(unit_text * grad_text_share, axis=1),
            loss_sum,
        ),
        ("mp", "pair"),
    )
    back_image = backward(unit_image, norm_image, grad_image_share, inner_image)
    back_text = backward(unit_text, norm_text, grad_text_share, inner_text)
    head_width = back_image.shape[1]
    image_term = lax.dot_general(
        image_features, back_image, (((0,), (0,)), ((), ())), preferred_element_type=jnp.float32
    )
    text_term = lax.dot_general(
        text_features, back_text, (((0,), (0,)), ((), ())), preferred_element_type=jnp.float32
    )
    head_sums = lax.psum_scatter(
        jnp.concatenate([image_term, text_term], axis=1), "dp", scatter_dimension=0, tiled=True
    )
    row_loss = loss_total / (block_rows * cycle_size)
    return (row_loss, head_sums[:, :head_width], head_sums[:, head_width:])


def solution(mesh):
    in_specs = (
        P(("groups", "dp"), None),
        P(("groups", "dp"), None),
        P(None, ("mp", "pair")),
        P(None, ("mp", "pair")),
        P(),
        P(),
    )
    out_specs = (
        P(("groups", "dp")),
        P(("groups", "dp"), ("mp", "pair")),
        P(("groups", "dp"), ("mp", "pair")),
    )
    return jax.shard_map(body, mesh=mesh, in_specs=in_specs, out_specs=out_specs, check_vma=False)
```

profile of v0, /device:TPU:0, one launch (start us, length us, event | category | flops | bytes accessed | tf_op | source)
XLA Modules:
  0.0 181.5 jit_solution(4514370448645126225)
XLA Ops:
  7.2 1.1 copy-done
  8.3 1.5 multiply_reduce_fusion.2
  9.8 0.4 multiply_reduce_fusion.3
  10.2 8.4 %all-reduce.1 = (f32[256]{0:T(256)S(1)}, f32[256]{0:T(256)S(1)}) all-reduce(f32[256]{0:T(256)S(1)} %get-tuple-element.383, f32[256]{0:T(256)S(1)} %get-tuple-element.385), channel_id=1, replica_groups=mesh['groups'=2,'dp'=4,'mp'=2,'pair'=2] {'mp','pair'}, use_global_device_ids=true, to_apply=%region_1.0 | all-reduce | flops 512 | bytes 4096 | tf_op jit(solution)/shard_map/psum | solution.py:30
  18.6 0.8 copy.31
  19.4 3.4 %all-to-all-start = ((bf16[4,64,288]{2,1,0:T(8,128)(2,1)}), bf16[4,64,288]{2,1,0:T(8,128)(2,1)S(1)}, u32[]{:S(2)}, u32[]{:S(2)}) async-start(bf16[4,64,288]{2,1,0:T(8,128)(2,1)} %bitcast), calls=%async_computation | async-start | bytes 393216 | tf_op jit(solution)/shard_map/all_to_all | solution.py:41
  23.6 9.0 %all_gather.3 = bf16[256,1152]{0,1:T(8,128)(2,1)} all-gather(bf16[256,288]{0,1:T(8,128)(2,1)S(1)} %fusion.12), channel_id=1, replica_groups=mesh['groups'=2,'dp'=4,'mp'=2,'pair'=2] {'mp','pair'}, dimensions={1}, use_global_device_ids=true | all-gather | bytes 737280 | tf_op jit(solution)/shard_map/all_gather | solution.py:40
  32.5 1.4 copy.33
  33.9 0.2 copy.32
  34.1 0.2 all_to_all.34
  34.3 1.1 broadcast_in_dim.45
  35.4 29.3 %while.22 = (s32[]{:T(128)}, bf16[64,1152]{1,0:T(8,128)(2,1)S(1)}, f32[4,64,1152]{2,1,0:T(8,128)}, f32[256,1152]{1,0:T(8,128)S(1)}, f32[256]{0:T(256)S(1)}, /*in...) while((s32[]{:T(128)}, bf16[64,1152]{1,0:T(8,128)(2,1)S(1)}, ...), condition=%wide.region_6.7_spmd.clone, body=%wide.region_4.6_spmd.clone.sunk | while | flops 114393360 | bytes 5215853 | solution.py:80
  35.4 1.6 collective-permute-start
  37.0 1.0 fusion.34
  38.0 0.6 convolution_add_fusion.2
  38.6 1.0 fusion.35
  39.6 3.8 %collective-permute-done = bf16[64,1152]{1,0:T(8,128)(2,1)S(1)} collective-permute-done((bf16[64,1152]{1,0:T(8,128)(2,1)S(1)}, bf16[64,1152]{1,0:T(8,128)(2,1)S(1)}, u32[]{:S(2)}, u32[]{:S(2)}) %collective-permute-start) | collective-permute-done | bytes 147488 | tf_op jit(solution)/shard_map/while/body/eval_jaxpr/ppermute | solution.py:12
  43.4 0.1 collective-permute-start
  43.5 1.0 fusion.34
  44.6 0.6 convolution_add_fusion.2
  45.1 1.0 fusion.35
  46.2 4.5 %collective-permute-done = bf16[64,1152]{1,0:T(8,128)(2,1)S(1)} collective-permute-done((bf16[64,1152]{1,0:T(8,128)(2,1)S(1)}, bf16[64,1152]{1,0:T(8,128)(2,1)S(1)}, u32[]{:S(2)}, u32[]{:S(2)}) %collective-permute-start) | collective-permute-done | bytes 147488 | tf_op jit(solution)/shard_map/while/body/eval_jaxpr/ppermute | solution.py:12
  50.8 1.0 fusion.34
  51.8 0.6 convolution_add_fusion.2
  52.4 1.0 fusion.35
  53.4 4.3 %collective-permute-done = bf16[64,1152]{1,0:T(8,128)(2,1)S(1)} collective-permute-done((bf16[64,1152]{1,0:T(8,128)(2,1)S(1)}, bf16[64,1152]{1,0:T(8,128)(2,1)S(1)}, u32[]{:S(2)}, u32[]{:S(2)}) %collective-permute-start) | collective-permute-done | bytes 147488 | tf_op jit(solution)/shard_map/while/body/eval_jaxpr/ppermute | solution.py:12
  57.8 1.0 fusion.34
  58.8 0.6 convolution_add_fusion.2
  59.4 1.0 fusion.35
  60.4 4.3 %collective-permute-done = bf16[64,1152]{1,0:T(8,128)(2,1)S(1)} collective-permute-done((bf16[64,1152]{1,0:T(8,128)(2,1)S(1)}, bf16[64,1152]{1,0:T(8,128)(2,1)S(1)}, u32[]{:S(2)}, u32[]{:S(2)}) %collective-permute-start) | collective-permute-done | bytes 147488 | tf_op jit(solution)/shard_map/while/body/eval_jaxpr/ppermute | solution.py:12
  64.7 1.4 copy.34
  66.1 28.9 %all_to_all.43 = f32[4,64,1152]{2,1,0:T(8,128)S(1)} all-to-all(f32[4,64,1152]{2,1,0:T(8,128)} %get-tuple-element.256), channel_id=1, replica_groups=mesh['groups'=2,'dp'=4,'mp'=2,'pair'=2] {'dp'}, dimensions={0} | all-to-all | bytes 2359296 | tf_op jit(solution)/shard_map/all_to_all | solution.py:84
  95.0 0.1 reduce_sum.64
  95.1 0.3 all_to_all.36
  95.4 10.0 %all_to_all.44 = f32[64,4,288]{2,0,1:T(8,128)S(1)} all-to-all(f32[64,4,288]{2,0,1:T(8,128)S(1)} %copy.35), channel_id=1, replica_groups=mesh['groups'=2,'dp'=4,'mp'=2,'pair'=2] {'mp','pair'}, dimensions={1} | all-to-all | bytes 589824 | tf_op jit(solution)/shard_map/all_to_all | solution.py:87
  105.4 0.1 copy.37
  105.6 0.1 multiply_reduce_fusion
  105.7 1.0 multiply_reduce_fusion.1
  106.7 5.8 %all-reduce = (f32[256]{0:T(256)S(1)}, f32[256]{0:T(256)S(1)}, f32[256]{0:T(256)S(1)}) all-reduce(f32[256]{0:T(256)S(1)} %get-tuple-element.254, f32[256]{0:T(256)S(1)} %multiply_reduce_fusion, f32[256]{0:T(256)S(1)} %multiply_reduce_fusion.1), channel_id=1, replica_groups=mesh['groups'=2,'dp'=4,'mp'=2,'pair'=2] {'mp','pair'}, use_global_device_ids=true, to_apply=%region_7.8 | all-reduce | flops 768 | bytes 6144 | tf_op jit(solution)/shard_map/psum | solution.py:90
  112.5 0.4 convolution_bitcast_fusion.1
  112.8 0.7 copy-done.4
  113.5 0.1 copy-done.5
  113.6 0.4 convolution_bitcast_fusion.2
  114.0 0.2 pad_maximum_fusion
  114.1 2.3 %copy.40 = f32[1152,576]{1,0:T(8,128)} copy(f32[1152,576]{0,1:T(8,128)S(1)} %pad_maximum_fusion) | data formatting | bytes 5308416
  116.5 0.6 broadcast_multiply_fusion
  117.1 55.4 %reduce-scatter.7.cloned.1.call-done = f32[288,576]{1,0:T(8,128)} async-done(((f32[1152,576]{1,0:T(8,128)}), f32[288,576]{1,0:T(8,128)}) %reduce-scatter.7.cloned.1.call-update) | async-done | bytes 663568
  172.5 2.2 %fusion.13 = (f32[288,288]{1,0:T(8,128)}, f32[288,288]{1,0:T(8,128)}) fusion(f32[288,576]{1,0:T(8,128)} %reduce-scatter.7.cloned.1.call-done), kind=kLoop, calls=%fused_computation.35 | loop fusion | bytes 1327104 | tf_op jit(solution)/shard_map/slice | solution.py:111
  (33 shorter events, 0.5 us)
Async XLA Ops:
  7.2 1.1 copy-start
  7.2 2.6 %copy-start.2 = (bf16[256,1152]{1,0:T(8,128)(2,1)S(1)}, bf16[256,1152]{1,0:T(8,128)(2,1)}, u32[]{:S(2)}) copy-start(bf16[256,1152]{1,0:T(8,128)(2,1)} %param.9) | copy-start | bytes 1769476
  7.2 2.6 %copy-start.1 = (bf16[1152,288]{0,1:T(8,128)(2,1)S(1)}, bf16[1152,288]{0,1:T(8,128)(2,1)}, u32[]{:S(2)}) copy-start(bf16[1152,288]{0,1:T(8,128)(2,1)} %param.11) | copy-start | bytes 1990660
  19.4 14.5 %all-to-all-start = ((bf16[4,64,288]{2,1,0:T(8,128)(2,1)}), bf16[4,64,288]{2,1,0:T(8,128)(2,1)S(1)}, u32[]{:S(2)}, u32[]{:S(2)}) async-start(bf16[4,64,288]{2,1,0:T(8,128)(2,1)} %bitcast), calls=%async_computation | async-start | bytes 393216 | tf_op jit(solution)/shard_map/all_to_all | solution.py:41
  22.8 82.9 %reduce-scatter.5.cloned.1.call-start = ((), (), s32[]{:S(2)}) async-start(), calls=%async_computation.5 | async-start | bytes 1474560 | tf_op jit(solution)/shard_map/reduce_scatter | solution.py:86
  35.4 8.0 %collective-permute-start = (bf16[64,1152]{1,0:T(8,128)(2,1)S(1)}, bf16[64,1152]{1,0:T(8,128)(2,1)S(1)}, u32[]{:S(2)}, u32[]{:S(2)}) collective-permute-start(bf16[64,1152]{1,0:T(8,128)(2,1)S(1)} %copy.51), channel_id=1, source_target_pairs={{12,0},{0,4},{4,8},{8,12},{13,1},{1,5},{5,9},{9,13},{14,2},{2,6},{... | collective-permute-start | bytes 442376 | tf_op jit(solution)/shard_map/while/body/eval_jaxpr/ppermute | solution.py:12
  43.4 7.2 %collective-permute-start = (bf16[64,1152]{1,0:T(8,128)(2,1)S(1)}, bf16[64,1152]{1,0:T(8,128)(2,1)S(1)}, u32[]{:S(2)}, u32[]{:S(2)}) collective-permute-start(bf16[64,1152]{1,0:T(8,128)(2,1)S(1)} %copy.51), channel_id=1, source_target_pairs={{12,0},{0,4},{4,8},{8,12},{13,1},{1,5},{5,9},{9,13},{14,2},{2,6},{... | collective-permute-start | bytes 442376 | tf_op jit(solution)/shard_map/while/body/eval_jaxpr/ppermute | solution.py:12
  50.7 7.0 %collective-permute-start = (bf16[64,1152]{1,0:T(8,128)(2,1)S(1)}, bf16[64,1152]{1,0:T(8,128)(2,1)S(1)}, u32[]{:S(2)}, u32[]{:S(2)}) collective-permute-start(bf16[64,1152]{1,0:T(8,128)(2,1)S(1)} %copy.51), channel_id=1, source_target_pairs={{12,0},{0,4},{4,8},{8,12},{13,1},{1,5},{5,9},{9,13},{14,2},{2,6},{... | collective-permute-start | bytes 442376 | tf_op jit(solution)/shard_map/while/body/eval_jaxpr/ppermute | solution.py:12
  57.7 7.0 %collective-permute-start = (bf16[64,1152]{1,0:T(8,128)(2,1)S(1)}, bf16[64,1152]{1,0:T(8,128)(2,1)S(1)}, u32[]{:S(2)}, u32[]{:S(2)}) collective-permute-start(bf16[64,1152]{1,0:T(8,128)(2,1)S(1)} %copy.51), channel_id=1, source_target_pairs={{12,0},{0,4},{4,8},{8,12},{13,1},{1,5},{5,9},{9,13},{14,2},{2,6},{... | collective-permute-start | bytes 442376 | tf_op jit(solution)/shard_map/while/body/eval_jaxpr/ppermute | solution.py:12
  66.1 106.4 %reduce-scatter.7.cloned.1.call-start = ((), (), s32[]{:S(2)}) async-start(), calls=%async_computation.6 | async-start | bytes 3686400
  95.4 17.0 %copy-start.3 = (bf16[256,1152]{1,0:T(8,128)(2,1)S(1)}, bf16[256,1152]{1,0:T(8,128)(2,1)}, u32[]{:S(2)}) copy-start(bf16[256,1152]{1,0:T(8,128)(2,1)} %param.9) | copy-start | bytes 1769476
  112.5 1.1 copy-start.4
  112.5 1.1 copy-start.5
Sparse Core Ops, SparseCore 0:
  66.2 23.2 reduce-scatter.4
  116.6 55.8 reduce-scatter.6
where the time goes:
time: 182 us
  waiting for transfers between devices  72.3 us (40%)
  blocking collectives  61.9 us (34%)
  between operations  14.9 us (8%)
  matrix products  13 us (7%)
  local copies, waits for them, and re-layouts  11.8 us (6%)
  starting transfers between devices  5.24 us (3%)
  other arithmetic  2.07 us (1%)
    unnamed x3, waiting for transfers between devices  55.4 us
    all_to_all x1, blocking collectives, body(): lax.all_to_all(store, 'dp', split_axis=0, concat_axis=0, tiled=True)  28.9 us
    ppermute x4, waiting for transfers between devices, from_behind(): return lax.ppermute(block, axis, route)  16.9 us
    all_to_all x1, blocking collectives, body(): lax.all_to_all(grad_text_home, ('mp', 'pair'), split_axis=1, concat_axis=...  9.97 us
    all_gather x1, blocking collectives, body(): full_image = lax.all_gather(emb_image, ('mp', 'pair'), axis=1, tiled=True)  8.96 us
    psum x1, blocking collectives, body(): lax.psum((jnp.sum(proj_image * proj_image, axis=1), jnp.sum(proj_text * p...  8.36 us
    psum x1, blocking collectives, body(): lax.psum((jnp.sum(unit_image * grad_image_share, axis=1), jnp.sum(unit_te...  5.76 us
    unnamed x14, local copies, waits for them, and re-layouts  5.54 us
  transfers between devices with their start and end apart: 7, of which 5 were waited for; matrix products, arithmetic and copies ran while one was open for 7% of the time, Pallas kernels for 0%

commit v1 on v0

v1 whole, which is shorter than its diff:
```python
import functools

import jax
import jax.numpy as jnp
from jax import lax
from jax.experimental import pallas as pl
from jax.experimental.pallas import tpu as pltpu
from jax.sharding import PartitionSpec as P

epsilon = 1e-06
f32 = jnp.float32
bf16 = jnp.bfloat16
MESH = pl.DeviceIdType.MESH


def dot_nt(a, b):
    return lax.dot_general(a, b, (((1,), (1,)), ((), ())), preferred_element_type=f32)


def dot_tn(a, b):
    return lax.dot_general(a, b, (((0,), (0,)), ((), ())), preferred_element_type=f32)


def dot_nn(a, b):
    return jnp.dot(a, b, preferred_element_type=f32)


def as_rows(first, second):
    lanes = lax.broadcasted_iota(jnp.int32, (first.shape[0], 128), 1)
    wide = jnp.where(lanes == 0, first, jnp.where(lanes == 1, second, 0.0))
    return wide.T[:8]


def as_columns(block):
    wide = jnp.concatenate([block, jnp.zeros((120, block.shape[1]), f32)], axis=0).T
    return wide[:, 0:1], wide[:, 1:2]


def kernel(
    n, mp, pair,
    scalars, xi, xt, hi, ht, xti, xtt,
    loss_out, gi_out, gt_out,
    unit_i, unit_t, image, text, tall, wall, gi_send, gi_recv, gt_send, gt_recv, own_gt,
    ts_send, ts_recv, stat_send, stat_recv, head_send, head_recv,
    s_send, s_recv, d_send, d_recv,
):
    shards = mp * pair
    rows = xi.shape[0]
    part = rows // shards
    width = hi.shape[1]
    my_d = lax.axis_index("dp")
    my_s = lax.axis_index("mp") * pair + lax.axis_index("pair")
    offsets = [0] + [((k + 1) // 2) * (1 if k % 2 else -1) % n for k in range(1, n)]

    def ahead(k):
        return lax.rem(my_d + offsets[k], n)

    def behind(k):
        return lax.rem(my_d + n - offsets[k], n)

    def shard_up(k):
        return lax.rem(my_s + k, shards)

    def shard_down(k):
        return lax.rem(my_s + shards - k, shards)

    def shard_id(s):
        return {"mp": s // pair, "pair": lax.rem(s, pair)}

    def to_shard(src, dst, stage, k, s):
        copy = pltpu.make_async_remote_copy(
            src_ref=src, dst_ref=dst, send_sem=s_send.at[stage, k], recv_sem=s_recv.at[stage, k],
            device_id=shard_id(s), device_id_type=MESH)
        copy.start()
        return copy

    def to_dp(src, dst, stage, k, d):
        copy = pltpu.make_async_remote_copy(
            src_ref=src, dst_ref=dst, send_sem=d_send.at[stage, k], recv_sem=d_recv.at[stage, k],
            device_id={"dp": d}, device_id_type=MESH)
        copy.start()
        return copy

    sent = []
    others = range(1, shards)
    peers = range(1, n)

    barrier = pltpu.get_barrier_semaphore()
    for k in others:
        pl.semaphore_signal(barrier, inc=1, device_id=shard_id(shard_up(k)), device_id_type=MESH)
    for k in peers:
        pl.semaphore_signal(barrier, inc=1, device_id={"dp": ahead(k)}, device_id_type=MESH)

    def stats_start(stage, first, second):
        stat_send[stage] = as_rows(first, second)
        return [
            to_shard(stat_send.at[stage], stat_recv.at[stage, k], stage, k, shard_up(k))
            for k in others
        ]

    def stats_total(stage, copies):
        total = stat_send[stage]
        for k, copy in zip(others, copies):
            copy.wait_recv()
            total = total + stat_recv[stage, k]
        sent.extend(copies)
        return total

    proj_i = dot_nn(xi[...], hi[...])
    proj_t = dot_nn(xt[...], ht[...])
    sq_i = jnp.sum(proj_i * proj_i, axis=1, keepdims=True)
    sq_t = jnp.sum(proj_t * proj_t, axis=1, keepdims=True)
    pl.semaphore_wait(barrier, shards - 1 + n - 1)
    total_i, total_t = as_columns(stats_total(0, stats_start(0, sq_i, sq_t)))
    norm_i = jnp.sqrt(total_i + epsilon)
    norm_t = jnp.sqrt(total_t + epsilon)
    unit_text = proj_t / norm_t
    unit_t[...] = unit_text
    text[...] = unit_text.astype(bf16).reshape(shards, part, width)
    text_copies = [
        to_shard(text.at[shard_up(k)], tall.at[0, k], 3, k, shard_up(k)) for k in others
    ]
    tall[0, 0] = text[my_s]
    unit_image = proj_i / norm_i
    unit_i[...] = unit_image
    image[0] = unit_image.astype(bf16)
    image_copies = [to_shard(image.at[0], image.at[k], 4, k, shard_up(k)) for k in others]

    for copy in text_copies:
        copy.wait_recv()
    tall_copies = [to_dp(tall.at[0], tall.at[k], 0, k, ahead(k)) for k in peers]
    for copy in image_copies:
        copy.wait_recv()
    sent += text_copies + image_copies + tall_copies

    scale = scalars[0]
    offset = scalars[1]
    row_ids = lax.broadcasted_iota(jnp.int32, (rows, part), 0)
    col_ids = lax.broadcasted_iota(jnp.int32, (rows, part), 1) + my_s * part
    loss = jnp.zeros((rows, 1), f32)
    gt_copies = []
    for k in range(n):
        if k:
            tall_copies[k - 1].wait_recv()
        dots = dot_nt(image[0], tall[k, 0])
        for j in others:
            dots = dots + dot_nt(image[j], tall[k, j])
        logits = scale * dots + offset
        if k == 0:
            flip = jnp.where(row_ids == col_ids, f32(-1.0), f32(1.0))
        else:
            flip = f32(1.0)
        z = flip * logits
        small = jnp.exp(-jnp.abs(z))
        loss = loss + jnp.sum(jnp.maximum(z, 0.0) + jnp.log1p(small), axis=1, keepdims=True)
        sigmoid = jnp.where(z >= 0, f32(1.0), small) / (1.0 + small)
        weights = (flip * sigmoid * (scale / rows)).astype(bf16)
        wall[:, k * part:(k + 1) * part] = weights
        for j in range(shards):
            update = dot_tn(weights, image[j])
            if k == 0:
                own_gt[j] = update
            else:
                gt_send[k, j] = update.astype(bf16)
        if k:
            gt_copies.append(to_dp(gt_send.at[k], gt_recv.at[k], 1, k, behind(k)))
    sent += gt_copies

    gi_copies = []
    for j in list(others) + [0]:
        grad = dot_nn(wall[...], tall[:, j].reshape(n * part, width))
        if j:
            gi_send[j] = grad.astype(bf16)
            gi_copies.append(to_shard(gi_send.at[j], gi_recv.at[j], 5, j, shard_down(j)))
    sent += gi_copies
    for j, copy in zip(others, gi_copies):
        copy.wait_recv()
        grad = grad + gi_recv[j].astype(f32)
    stat_copies = stats_start(1, jnp.sum(unit_i[...] * grad, axis=1, keepdims=True), loss)
    total = stats_total(1, stat_copies)
    loss_out[...] = total[1:2] / (rows * n)
    inner, _ = as_columns(total)
    back_i = ((grad - unit_i[...] * inner) / norm_i).astype(bf16)

    def head_terms(which, x, back):
        copies = []
        for k in peers:
            head_send[which, k] = dot_nn(x[ahead(k)], back).astype(bf16)
            copies.append(to_dp(
                head_send.at[which, k], head_recv.at[which, k], 2 + which, k, ahead(k)))
        sent.extend(copies)
        return dot_nn(x[my_d], back), copies

    head_i, head_i_copies = head_terms(0, xti, back_i)

    for copy in gt_copies:
        copy.wait_recv()
    ts_copies = []
    for j in list(others) + [0]:
        share = own_gt[j]
        for k in peers:
            share = share + gt_recv[k, j].astype(f32)
        if j:
            ts_send[j] = share.astype(bf16)
            ts_copies.append(to_shard(ts_send.at[j], ts_recv.at[my_s], 6, j, shard_down(j)))
        else:
            ts_recv[my_s] = share.astype(bf16)
    sent += ts_copies
    for copy in ts_copies:
        copy.wait_send()
    for j in others:
        pltpu.make_async_remote_copy(
            src_ref=ts_send.at[j], dst_ref=ts_recv.at[shard_up(j)], send_sem=s_send.at[6, j],
            recv_sem=s_recv.at[6, j], device_id=shard_id(shard_down(j)), device_id_type=MESH,
        ).wait_recv()
    grad_t = ts_recv[...].reshape(rows, width).astype(f32)
    inner_t = jnp.sum(unit_t[...] * grad_t, axis=1, keepdims=True)
    inner_t, _ = as_columns(stats_total(2, stats_start(2, inner_t, inner_t)))
    back_t = ((grad_t - unit_t[...] * inner_t) / norm_t).astype(bf16)
    head_t, head_t_copies = head_terms(1, xtt, back_t)

    high = gi_out.shape[0]
    for which, value, copies, out in (
        (0, head_i, head_i_copies, gi_out), (1, head_t, head_t_copies, gt_out)
    ):
        for k, copy in zip(peers, copies):
            copy.wait_recv()
            value = value + head_recv[which, k].astype(f32)
        out[...] = value[:high]
    for copy in sent:
        if not any(copy is done for done in ts_copies):
            copy.wait_send()


def body(image_features, text_features, image_head, text_head, log_scale, bias):
    rows, depth = image_features.shape
    width = image_head.shape[1]
    n, mp, pair = lax.axis_size("dp"), lax.axis_size("mp"), lax.axis_size("pair")
    shards = mp * pair
    part = rows // shards
    high = depth // n
    padded = -(-high // 16) * 16

    def turned(features):
        blocks = features.T.reshape(n, high, rows)
        return jnp.pad(blocks, ((0, 0), (0, padded - high), (0, 0)))

    scalars = jnp.concatenate([jnp.exp(log_scale), bias])
    vmem = pl.BlockSpec(memory_space=pltpu.VMEM)
    row_loss, gi, gt = pl.pallas_call(
        functools.partial(kernel, n, mp, pair),
        out_shape=(
            jax.ShapeDtypeStruct((1, rows), f32),
            jax.ShapeDtypeStruct((high, width), f32),
            jax.ShapeDtypeStruct((high, width), f32),
        ),
        in_specs=[pl.BlockSpec(memory_space=pltpu.SMEM)] + [vmem] * 6,
        out_specs=(vmem, vmem, vmem),
        scratch_shapes=[
            pltpu.VMEM((rows, width), f32),
            pltpu.VMEM((rows, width), f32),
            pltpu.VMEM((shards, rows, width), bf16),
            pltpu.VMEM((shards, part, width), bf16),
            pltpu.VMEM((n, shards, part, width), bf16),
            pltpu.VMEM((rows, n * part), bf16),
            pltpu.VMEM((shards, rows, width), bf16),
            pltpu.VMEM((shards, rows, width), bf16),
            pltpu.VMEM((n, shards, part, width), bf16),
            pltpu.VMEM((n, shards, part, width), bf16),
            pltpu.VMEM((shards, part, width), f32),
            pltpu.VMEM((shards, part, width), bf16),
            pltpu.VMEM((shards, part, width), bf16),
            pltpu.VMEM((3, 8, rows), f32),
            pltpu.VMEM((3, shards, 8, rows), f32),
            pltpu.VMEM((2, n, padded, width), bf16),
            pltpu.VMEM((2, n, padded, width), bf16),
            pltpu.SemaphoreType.DMA((7, shards)),
            pltpu.SemaphoreType.DMA((7, shards)),
            pltpu.SemaphoreType.DMA((4, n)),
            pltpu.SemaphoreType.DMA((4, n)),
        ],
        compiler_params=pltpu.CompilerParams(
            collective_id=0, has_side_effects=True, vmem_limit_bytes=56 * 1024 * 1024
        ),
    )(
        scalars, image_features, text_features, image_head, text_head,
        turned(image_features), turned(text_features),
    )
    return row_loss.reshape(rows), gi, gt


def solution(mesh):
    in_specs = (
        P(("groups", "dp"), None),
        P(("groups", "dp"), None),
        P(None, ("mp", "pair")),
        P(None, ("mp", "pair")),
        P(),
        P(),
    )
    out_specs = (
        P(("groups", "dp")),
        P(("groups", "dp"), ("mp", "pair")),
        P(("groups", "dp"), ("mp", "pair")),
    )
    return jax.shard_map(body, mesh=mesh, in_specs=in_specs, out_specs=out_specs, check_vma=False)
```

time: 182 us -> 101 us (0.55)
  Pallas kernels: 0 us -> 89 us
  waiting for transfers between devices: 72.3 us -> 0 us
  blocking collectives: 61.9 us -> 0 us
  matrix products: 13 us -> 0 us
  between operations: 14.9 us -> 1.99 us
  starting transfers between devices: 5.24 us -> 0 us
  local copies, waits for them, and re-layouts: 11.8 us -> 9.62 us
    pallas_call x0 -> x1, Pallas kernels: none -> 89 us  [body(): pl.pallas_call(functools.partial(kernel, n, mp, pair), out_shape=(jax.Sha...]
    unnamed x3 -> x0, waiting for transfers between devices: 55.4 us -> none
    all_to_all x2 -> x0, blocking collectives: 38.9 us -> none  [the longest x1 28.9 us: body(): lax.all_to_all(store, 'dp', split_axis=0, concat_axis=0, tiled=True)]
    ppermute x4 -> x0, waiting for transfers between devices: 16.9 us -> none  [from_behind(): return lax.ppermute(block, axis, route)]
    psum x2 -> x0, blocking collectives: 14.1 us -> none  [the longest x1 8.36 us: body(): lax.psum((jnp.sum(proj_image * proj_image, axis=1), jnp.sum(proj_text * p...]
    dot_general x16 -> x0, matrix products: 13 us -> none  [the longest x4 4.08 us: compare(): lax.dot_general(full_image, visiting, (((1,), (1,)), ((), ())), preferred...]
    all_gather x1 -> x0, blocking collectives: 8.96 us -> none  [body(): full_image = lax.all_gather(emb_image, ('mp', 'pair'), axis=1, tiled=True)]
    all_to_all x1 -> x0, starting transfers between devices: 3.37 us -> none  [body(): lax.all_to_all(emb_text, ('mp', 'pair'), split_axis=0, concat_axis=1, til...]
  transfers between devices with their start and end apart: 7 -> 0, of which waited for: 5 -> 0; matrix products, arithmetic and copies ran while one was open for 7% -> 0% of each run, Pallas kernels for 0% -> 0%
where the time goes in v1:
time: 101 us
  Pallas kernels  89 us (88%)
  local copies, waits for them, and re-layouts  9.62 us (10%)
  between operations  1.99 us (2%)
    pallas_call x1, Pallas kernels, body(): pl.pallas_call(functools.partial(kernel, n, mp, pair), out_shape=(jax.Sha...  89 us
    unnamed x15, local copies, waits for them, and re-layouts  6.36 us
    transpose x2, local copies, waits for them, and re-layouts, turned(): blocks = features.T.reshape(n, high, rows)  3.26 us

profile of v1, /device:TPU:0, one launch (start us, length us, event | category | flops | bytes accessed | tf_op | source)
XLA Modules:
  0.0 101.2 jit_solution(9121743196120671555)
XLA Ops:
  2.0 0.6 pad_maximum_fusion.scalars
  2.5 0.0 copy-start
  2.5 2.2 %copy.10 = bf16[1152,256]{1,0:T(8,128)(2,1)} copy(bf16[1152,256]{0,1:T(8,128)(2,1)} %bitcast.6) | data formatting | bytes 1179648 | tf_op jit(solution)/shard_map/transpose | solution.py:245
  4.7 0.0 copy-start.1
  4.7 0.0 copy-done
  4.7 1.1 %copy.9 = bf16[1152,256]{1,0:T(8,128)(2,1)} copy(bf16[1152,256]{0,1:T(8,128)(2,1)S(1)} %bitcast.5) | data formatting | bytes 1179648 | tf_op jit(solution)/shard_map/transpose | solution.py:245
  5.8 0.0 copy-done.1
  5.8 0.0 copy-start.2
  5.8 1.2 %copy.11.hi = bf16[1152,288]{1,0:T(8,128)(2,1)} copy(bf16[1152,288]{0,1:T(8,128)(2,1)S(1)} %copy-done.1) | data formatting | bytes 1327104 | tf_op args[2]
  7.1 0.0 copy-done.2
  7.1 1.3 %copy.12.ht = bf16[1152,288]{1,0:T(8,128)(2,1)} copy(bf16[1152,288]{0,1:T(8,128)(2,1)S(1)} %copy-done.2) | data formatting | bytes 1327104 | tf_op args[3]
  8.3 89.0 %shard_map.85 = (f32[1,256]{1,0:T(1,128)}, f32[288,288]{1,0:T(8,128)}, f32[288,288]{1,0:T(8,128)}) custom-call(f32[2]{0:T(128)} %pad_maximum_fusion.scalars, bf16[256,1152]{1,0:T(8,128)(2,1)} %xi.1, bf16[256,1152]{1,0:T(8,128)(2,1)} %xt.1, bf16[1152,288]{1,0:T(8,128)(2,1)} %copy.11.hi, bf16[1152,288]{1,0:T(8,128)(2,1)} %copy.12.ht, ...), custom_call_target="tpu_custom_call" | custom-call | tf_op jit(solution)/shard_map/pallas_call | solution.py:250
  97.4 0.0 copy-start.4
  97.4 0.6 copy-done.4
  98.0 0.6 copy.18
  98.6 0.0 copy-start.3
  98.6 1.9 %copy.19 = f32[288,288]{1,0:T(8,128)} copy(f32[288,288]{1,0:T(8,128)} %get-tuple-element.13) | data formatting | bytes 663552
  100.4 0.0 copy-done.3
  100.4 0.8 copy.20
Async XLA Ops:
  2.5 2.2 %copy-start = (bf16[256,1152]{1,0:T(8,128)(2,1)S(1)}, bf16[256,1152]{1,0:T(8,128)(2,1)}, u32[]{:S(2)}) copy-start(bf16[256,1152]{1,0:T(8,128)(2,1)} %xi.1) | copy-start | bytes 1769476
  4.7 1.1 %copy-start.1 = (bf16[1152,288]{0,1:T(8,128)(2,1)S(1)}, bf16[1152,288]{0,1:T(8,128)(2,1)}, u32[]{:S(2)}) copy-start(bf16[1152,288]{0,1:T(8,128)(2,1)} %param.8) | copy-start | bytes 1990660
  5.8 1.2 %copy-start.2 = (bf16[1152,288]{0,1:T(8,128)(2,1)S(1)}, bf16[1152,288]{0,1:T(8,128)(2,1)}, u32[]{:S(2)}) copy-start(bf16[1152,288]{0,1:T(8,128)(2,1)} %param.9) | copy-start | bytes 1990660
  97.4 0.7 copy-start.4
  98.6 1.9 %copy-start.3 = (f32[288,288]{1,0:T(8,128)S(1)}, f32[288,288]{1,0:T(8,128)}, u32[]{:S(2)}) copy-start(f32[288,288]{1,0:T(8,128)} %get-tuple-element.14) | copy-start | bytes 995332

commit v2 on v1

--- a/solution.py
+++ b/solution.py
@@ -36,18 +36,41 @@
     return wide[:, 0:1], wide[:, 1:2]
 
 
+def packing(width):
+    main = width // 128 * 128
+    rest = width - main
+
+    def groups(padded, high):
+        if not rest:
+            return []
+        step = tail_rows(padded, width)
+        starts = range(0, high, step)
+        return [
+            (low, min(low + step, high), j * rest, (j + 1) * rest) for j, low in enumerate(starts)
+        ]
+
+    return main, groups
+
+
+def tail_rows(padded, width):
+    main = width // 128 * 128
+    rest = width - main
+    return -(-padded // (main // rest * 8)) * 8 if rest else 0
+
+
 def kernel(
     n, mp, pair,
-    scalars, xi, xt, hi, ht, xti, xtt,
+    scalars, xi, xt, hi, ht,
     loss_out, gi_out, gt_out,
-    unit_i, unit_t, image, text, tall, wall, gi_send, gi_recv, gt_send, gt_recv, own_gt,
+    unit_i, unit_t, image, text, pieces, wide_image, turned, tall, wall, gi_send, gi_recv, gt_send, gt_recv, own_gt,
     ts_send, ts_recv, stat_send, stat_recv, head_send, head_recv,
     s_send, s_recv, d_send, d_recv,
 ):
     shards = mp * pair
     rows = xi.shape[0]
     part = rows // shards
-    width = hi.shape[1]
+    width = hi.shape[0]
+    high = gi_out.shape[0]
     my_d = lax.axis_index("dp")
     my_s = lax.axis_index("mp") * pair + lax.axis_index("pair")
     offsets = [0] + [((k + 1) // 2) * (1 if k % 2 else -1) % n for k in range(1, n)]
@@ -106,8 +129,8 @@
         sent.extend(copies)
         return total
 
-    proj_i = dot_nn(xi[...], hi[...])
-    proj_t = dot_nn(xt[...], ht[...])
+    proj_i = dot_nt(xi[...], hi[...])
+    proj_t = dot_nt(xt[...], ht[...])
     sq_i = jnp.sum(proj_i * proj_i, axis=1, keepdims=True)
     sq_t = jnp.sum(proj_t * proj_t, axis=1, keepdims=True)
     pl.semaphore_wait(barrier, shards - 1 + n - 1)
@@ -118,19 +141,26 @@
     unit_t[...] = unit_text
     text[...] = unit_text.astype(bf16).reshape(shards, part, width)
     text_copies = [
-        to_shard(text.at[shard_up(k)], tall.at[0, k], 3, k, shard_up(k)) for k in others
+        to_shard(text.at[shard_up(k)], pieces.at[k], 3, k, shard_up(k)) for k in others
     ]
-    tall[0, 0] = text[my_s]
+    tall[0, :, :width] = text[my_s]
     unit_image = proj_i / norm_i
     unit_i[...] = unit_image
     image[0] = unit_image.astype(bf16)
     image_copies = [to_shard(image.at[0], image.at[k], 4, k, shard_up(k)) for k in others]
 
-    for copy in text_copies:
+    for k, copy in zip(others, text_copies):
         copy.wait_recv()
+        tall[0, :, k * width:(k + 1) * width] = pieces[k]
     tall_copies = [to_dp(tall.at[0], tall.at[k], 0, k, ahead(k)) for k in peers]
-    for copy in image_copies:
+    wide_image[:, :width] = image[0]
+    for which, x in enumerate((xi, xt)):
+        across = x[...].T
+        for e in range(n):
+            turned[which, e, :high] = across[e * high:(e + 1) * high]
+    for k, copy in zip(others, image_copies):
         copy.wait_recv()
+        wide_image[:, k * width:(k + 1) * width] = image[k]
     sent += text_copies + image_copies + tall_copies
 
     scale = scalars[0]
@@ -142,9 +172,7 @@
     for k in range(n):
         if k:
             tall_copies[k - 1].wait_recv()
-        dots = dot_nt(image[0], tall[k, 0])
-        for j in others:
-            dots = dots + dot_nt(image[j], tall[k, j])
+        dots = dot_nt(wide_image[...], tall[k])
         logits = scale * dots + offset
         if k == 0:
             flip = jnp.where(row_ids == col_ids, f32(-1.0), f32(1.0))
@@ -156,19 +184,18 @@
         sigmoid = jnp.where(z >= 0, f32(1.0), small) / (1.0 + small)
         weights = (flip * sigmoid * (scale / rows)).astype(bf16)
         wall[:, k * part:(k + 1) * part] = weights
-        for j in range(shards):
-            update = dot_tn(weights, image[j])
-            if k == 0:
-                own_gt[j] = update
-            else:
-                gt_send[k, j] = update.astype(bf16)
-        if k:
+        update = dot_tn(weights, wide_image[...])
+        if k == 0:
+            own_gt[...] = update
+        else:
+            gt_send[k] = update.astype(bf16)
             gt_copies.append(to_dp(gt_send.at[k], gt_recv.at[k], 1, k, behind(k)))
     sent += gt_copies
 
     gi_copies = []
+    grad_all = dot_nn(wall[...], tall[...].reshape(n * part, shards * width))
     for j in list(others) + [0]:
-        grad = dot_nn(wall[...], tall[:, j].reshape(n * part, width))
+        grad = grad_all[:, j * width:(j + 1) * width]
         if j:
             gi_send[j] = grad.astype(bf16)
             gi_copies.append(to_shard(gi_send.at[j], gi_recv.at[j], 5, j, shard_down(j)))
@@ -182,24 +209,31 @@
     inner, _ = as_columns(total)
     back_i = ((grad - unit_i[...] * inner) / norm_i).astype(bf16)
 
-    def head_terms(which, x, back):
+    main, groups = packing(width)
+    padded = turned.shape[2]
+
+    def head_terms(which, back):
         copies = []
         for k in peers:
-            head_send[which, k] = dot_nn(x[ahead(k)], back).astype(bf16)
+            term = dot_nn(turned[which, ahead(k)], back).astype(bf16)
+            head_send[which, k, :padded] = term[:, :main]
+            for low, top, left, right in groups(padded, padded):
+                head_send[which, k, padded:padded + top - low, left:right] = term[low:top, main:]
             copies.append(to_dp(
                 head_send.at[which, k], head_recv.at[which, k], 2 + which, k, ahead(k)))
         sent.extend(copies)
-        return dot_nn(x[my_d], back), copies
-
-    head_i, head_i_copies = head_terms(0, xti, back_i)
+        return dot_nn(turned[which, my_d], back), copies
+
+    head_i, head_i_copies = head_terms(0, back_i)
 
     for copy in gt_copies:
         copy.wait_recv()
     ts_copies = []
+    share_all = own_gt[...]
+    for k in peers:
+        share_all = share_all + gt_recv[k].astype(f32)
     for j in list(others) + [0]:
-        share = own_gt[j]
-        for k in peers:
-            share = share + gt_recv[k, j].astype(f32)
+        share = share_all[:, j * width:(j + 1) * width]
         if j:
             ts_send[j] = share.astype(bf16)
             ts_copies.append(to_shard(ts_send.at[j], ts_recv.at[my_s], 6, j, shard_down(j)))
@@ -217,16 +251,19 @@
     inner_t = jnp.sum(unit_t[...] * grad_t, axis=1, keepdims=True)
     inner_t, _ = as_columns(stats_total(2, stats_start(2, inner_t, inner_t)))
     back_t = ((grad_t - unit_t[...] * inner_t) / norm_t).astype(bf16)
-    head_t, head_t_copies = head_terms(1, xtt, back_t)
-
-    high = gi_out.shape[0]
+    head_t, head_t_copies = head_terms(1, back_t)
+
     for which, value, copies, out in (
         (0, head_i, head_i_copies, gi_out), (1, head_t, head_t_copies, gt_out)
     ):
+        landed = jnp.zeros(head_recv.shape[2:], f32)
         for k, copy in zip(peers, copies):
             copy.wait_recv()
-            value = value + head_recv[which, k].astype(f32)
-        out[...] = value[:high]
+            landed = landed + head_recv[which, k].astype(f32)
+        out[:, :main] = value[:high, :main] + landed[:high]
+        for low, top, left, right in groups(padded, high):
+            out[low:top, main:] = (
+                value[low:top, main:] + landed[padded:padded + top - low, left:right])
     for copy in sent:
         if not any(copy is done for done in ts_copies):
             copy.wait_send()
@@ -241,10 +278,9 @@
     high = depth // n
     padded = -(-high // 16) * 16
 
-    def turned(features):
-        blocks = features.T.reshape(n, high, rows)
-        return jnp.pad(blocks, ((0, 0), (0, padded - high), (0, 0)))
-
+    wide = shards * width
+    tail = -(-tail_rows(padded, width) // 16) * 16
+    main = packing(width)[0]
     scalars = jnp.concatenate([jnp.exp(log_scale), bias])
     vmem = pl.BlockSpec(memory_space=pltpu.VMEM)
     row_loss, gi, gt = pl.pallas_call(
@@ -254,26 +290,29 @@
             jax.ShapeDtypeStruct((high, width), f32),
             jax.ShapeDtypeStruct((high, width), f32),
         ),
-        in_specs=[pl.BlockSpec(memory_space=pltpu.SMEM)] + [vmem] * 6,
+        in_specs=[pl.BlockSpec(memory_space=pltpu.SMEM)] + [vmem] * 4,
         out_specs=(vmem, vmem, vmem),
         scratch_shapes=[
             pltpu.VMEM((rows, width), f32),
             pltpu.VMEM((rows, width), f32),
             pltpu.VMEM((shards, rows, width), bf16),
             pltpu.VMEM((shards, part, width), bf16),
-            pltpu.VMEM((n, shards, part, width), bf16),
+            pltpu.VMEM((shards, part, width), bf16),
+            pltpu.VMEM((rows, wide), bf16),
+            pltpu.VMEM((2, n, padded, rows), bf16),
+            pltpu.VMEM((n, part, wide), bf16),
             pltpu.VMEM((rows, n * part), bf16),
             pltpu.VMEM((shards, rows, width), bf16),
             pltpu.VMEM((shards, rows, width), bf16),
-            pltpu.VMEM((n, shards, part, width), bf16),
-            pltpu.VMEM((n, shards, part, width), bf16),
-            pltpu.VMEM((shards, part, width), f32),
+            pltpu.VMEM((n, part, wide), bf16),
+            pltpu.VMEM((n, part, wide), bf16),
+            pltpu.VMEM((part, wide), f32),
             pltpu.VMEM((shards, part, width), bf16),
             pltpu.VMEM((shards, part, width), bf16),
             pltpu.VMEM((3, 8, rows), f32),
             pltpu.VMEM((3, shards, 8, rows), f32),
-            pltpu.VMEM((2, n, padded, width), bf16),
-            pltpu.VMEM((2, n, padded, width), bf16),
+            pltpu.VMEM((2, n, padded + tail, main), bf16),
+            pltpu.VMEM((2, n, padded + tail, main), bf16),
             pltpu.SemaphoreType.DMA((7, shards)),
             pltpu.SemaphoreType.DMA((7, shards)),
             pltpu.SemaphoreType.DMA((4, n)),
@@ -283,8 +322,7 @@
             collective_id=0, has_side_effects=True, vmem_limit_bytes=56 * 1024 * 1024
         ),
     )(
-        scalars, image_features, text_features, image_head, text_head,
-        turned(image_features), turned(text_features),
+        scalars, image_features, text_features, image_head.T, text_head.T,
     )
     return row_loss.reshape(rows), gi, gt
 

time: 101 us -> 82 us (0.81)
  Pallas kernels: 89 us -> 75.4 us
  local copies, waits for them, and re-layouts: 9.62 us -> 3.85 us
    pallas_call x1, Pallas kernels: 89 us -> 75.4 us  [body(): pl.pallas_call(functools.partial(kernel, n, mp, pair), out_shape=(jax.Sha...]
    transpose x2 -> x0, local copies, waits for them, and re-layouts: 3.26 us -> none  [turned(): blocks = features.T.reshape(n, high, rows)]
    unnamed x15 -> x7, local copies, waits for them, and re-layouts: 6.36 us -> 3.85 us
where the time goes in v2:
time: 82 us; the launch traced here: 81.8 us
  Pallas kernels  75.4 us (92%)
  local copies, waits for them, and re-layouts  3.85 us (5%)
  between operations  1.98 us (2%)
    pallas_call x1, Pallas kernels, body(): pl.pallas_call(functools.partial(kernel, n, mp, pair), out_shape=(jax.Sha...  75.4 us
    unnamed x7, local copies, waits for them, and re-layouts  3.85 us

profile of v2, /device:TPU:0, one launch (start us, length us, event | category | flops | bytes accessed | tf_op | source)
XLA Modules:
  0.0 81.8 jit_solution(3415874337549328976)
XLA Ops:
  2.0 0.6 pad_maximum_fusion.scalars
  2.5 75.4 %shard_map.85 = (f32[1,256]{1,0:T(1,128)}, f32[288,288]{1,0:T(8,128)}, f32[288,288]{1,0:T(8,128)}) custom-call(f32[2]{0:T(128)} %pad_maximum_fusion.scalars, bf16[256,1152]{1,0:T(8,128)(2,1)} %xi.1, bf16[256,1152]{1,0:T(8,128)(2,1)} %xt.1, bf16[288,1152]{1,0:T(8,128)(2,1)} %bitcast.3, bf16[288,1152]{1,0:T(8,128)(2,1)} %bitcast.4), custom_call_target="tpu_custom_call" | custom-call | tf_op jit(solution)/shard_map/pallas_call | solution.py:286
  77.9 0.0 copy-start.1
  77.9 0.7 copy-done.1
  78.6 0.6 copy.14
  79.2 0.0 copy-start
  79.2 1.9 %copy.15 = f32[288,288]{1,0:T(8,128)} copy(f32[288,288]{1,0:T(8,128)} %get-tuple-element.13) | data formatting | bytes 663552
  81.0 0.0 copy-done
  81.0 0.8 copy.16
Async XLA Ops:
  77.9 0.7 copy-start.1
  79.2 1.9 %copy-start = (f32[288,288]{1,0:T(8,128)S(1)}, f32[288,288]{1,0:T(8,128)}, u32[]{:S(2)}) copy-start(f32[288,288]{1,0:T(8,128)} %get-tuple-element.14) | copy-start | bytes 995332

commit v3 on v2

--- a/solution.py
+++ b/solution.py
@@ -60,7 +60,7 @@
 
 def kernel(
     n, mp, pair,
-    scalars, xi, xt, hi, ht,
+    log_scale, bias, xi, xt, hi, ht,
     loss_out, gi_out, gt_out,
     unit_i, unit_t, image, text, pieces, wide_image, turned, tall, wall, gi_send, gi_recv, gt_send, gt_recv, own_gt,
     ts_send, ts_recv, stat_send, stat_recv, head_send, head_recv,
@@ -163,11 +163,12 @@
         wide_image[:, k * width:(k + 1) * width] = image[k]
     sent += text_copies + image_copies + tall_copies
 
-    scale = scalars[0]
-    offset = scalars[1]
+    scale = jnp.exp(jnp.full((1, part), log_scale[0], f32))
+    offset = bias[0]
     row_ids = lax.broadcasted_iota(jnp.int32, (rows, part), 0)
     col_ids = lax.broadcasted_iota(jnp.int32, (rows, part), 1) + my_s * part
     loss = jnp.zeros((rows, 1), f32)
+    inner = jnp.zeros((rows, 1), f32)
     gt_copies = []
     for k in range(n):
         if k:
@@ -183,6 +184,7 @@
         loss = loss + jnp.sum(jnp.maximum(z, 0.0) + jnp.log1p(small), axis=1, keepdims=True)
         sigmoid = jnp.where(z >= 0, f32(1.0), small) / (1.0 + small)
         weights = (flip * sigmoid * (scale / rows)).astype(bf16)
+        inner = inner + jnp.sum(weights.astype(f32) * dots, axis=1, keepdims=True)
         wall[:, k * part:(k + 1) * part] = weights
         update = dot_tn(weights, wide_image[...])
         if k == 0:
@@ -191,6 +193,7 @@
             gt_send[k] = update.astype(bf16)
             gt_copies.append(to_dp(gt_send.at[k], gt_recv.at[k], 1, k, behind(k)))
     sent += gt_copies
+    stat_copies = stats_start(1, inner, loss)
 
     gi_copies = []
     grad_all = dot_nn(wall[...], tall[...].reshape(n * part, shards * width))
@@ -203,7 +206,6 @@
     for j, copy in zip(others, gi_copies):
         copy.wait_recv()
         grad = grad + gi_recv[j].astype(f32)
-    stat_copies = stats_start(1, jnp.sum(unit_i[...] * grad, axis=1, keepdims=True), loss)
     total = stats_total(1, stat_copies)
     loss_out[...] = total[1:2] / (rows * n)
     inner, _ = as_columns(total)
@@ -232,13 +234,19 @@
     share_all = own_gt[...]
     for k in peers:
         share_all = share_all + gt_recv[k].astype(f32)
+    inner_t = jnp.sum(tall[0].astype(f32) * share_all, axis=1, keepdims=True)
+    rounded = inner_t.astype(bf16).astype(f32)
+    columns = lax.broadcasted_iota(jnp.int32, (part, 2), 1)
+    extra = jnp.where(columns == 0, rounded, inner_t - rounded).astype(bf16)
     for j in list(others) + [0]:
         share = share_all[:, j * width:(j + 1) * width]
         if j:
-            ts_send[j] = share.astype(bf16)
+            ts_send[j, :, :width] = share.astype(bf16)
+            ts_send[j, :, width:] = extra
             ts_copies.append(to_shard(ts_send.at[j], ts_recv.at[my_s], 6, j, shard_down(j)))
         else:
-            ts_recv[my_s] = share.astype(bf16)
+            ts_recv[my_s, :, :width] = share.astype(bf16)
+            ts_recv[my_s, :, width:] = extra
     sent += ts_copies
     for copy in ts_copies:
         copy.wait_send()
@@ -247,9 +255,9 @@
             src_ref=ts_send.at[j], dst_ref=ts_recv.at[shard_up(j)], send_sem=s_send.at[6, j],
             recv_sem=s_recv.at[6, j], device_id=shard_id(shard_down(j)), device_id_type=MESH,
         ).wait_recv()
-    grad_t = ts_recv[...].reshape(rows, width).astype(f32)
-    inner_t = jnp.sum(unit_t[...] * grad_t, axis=1, keepdims=True)
-    inner_t, _ = as_columns(stats_total(2, stats_start(2, inner_t, inner_t)))
+    landed_t = ts_recv[...].reshape(rows, width + 2).astype(f32)
+    grad_t = landed_t[:, :width]
+    inner_t = landed_t[:, width:width + 1] + landed_t[:, width + 1:]
     back_t = ((grad_t - unit_t[...] * inner_t) / norm_t).astype(bf16)
     head_t, head_t_copies = head_terms(1, back_t)
 
@@ -269,6 +277,12 @@
             copy.wait_send()
 
 
+def hand_over(loss, gi, gt, loss_out, gi_out, gt_out):
+    loss_out[...] = loss[...]
+    gi_out[...] = gi[...]
+    gt_out[...] = gt[...]
+
+
 def body(image_features, text_features, image_head, text_head, log_scale, bias):
     rows, depth = image_features.shape
     width = image_head.shape[1]
@@ -281,16 +295,16 @@
     wide = shards * width
     tail = -(-tail_rows(padded, width) // 16) * 16
     main = packing(width)[0]
-    scalars = jnp.concatenate([jnp.exp(log_scale), bias])
+    smem = pl.BlockSpec(memory_space=pltpu.SMEM)
     vmem = pl.BlockSpec(memory_space=pltpu.VMEM)
-    row_loss, gi, gt = pl.pallas_call(
+    results = pl.pallas_call(
         functools.partial(kernel, n, mp, pair),
         out_shape=(
             jax.ShapeDtypeStruct((1, rows), f32),
             jax.ShapeDtypeStruct((high, width), f32),
             jax.ShapeDtypeStruct((high, width), f32),
         ),
-        in_specs=[pl.BlockSpec(memory_space=pltpu.SMEM)] + [vmem] * 4,
+        in_specs=[smem, smem] + [vmem] * 4,
         out_specs=(vmem, vmem, vmem),
         scratch_shapes=[
             pltpu.VMEM((rows, width), f32),
@@ -307,10 +321,10 @@
             pltpu.VMEM((n, part, wide), bf16),
             pltpu.VMEM((n, part, wide), bf16),
             pltpu.VMEM((part, wide), f32),
-            pltpu.VMEM((shards, part, width), bf16),
-            pltpu.VMEM((shards, part, width), bf16),
-            pltpu.VMEM((3, 8, rows), f32),
-            pltpu.VMEM((3, shards, 8, rows), f32),
+            pltpu.VMEM((shards, part, width + 2), bf16),
+            pltpu.VMEM((shards, part, width + 2), bf16),
+            pltpu.VMEM((2, 8, rows), f32),
+            pltpu.VMEM((2, shards, 8, rows), f32),
             pltpu.VMEM((2, n, padded + tail, main), bf16),
             pltpu.VMEM((2, n, padded + tail, main), bf16),
             pltpu.SemaphoreType.DMA((7, shards)),
@@ -322,8 +336,14 @@
             collective_id=0, has_side_effects=True, vmem_limit_bytes=56 * 1024 * 1024
         ),
     )(
-        scalars, image_features, text_features, image_head.T, text_head.T,
+        log_scale, bias, image_features, text_features, image_head.T, text_head.T,
     )
+    row_loss, gi, gt = pl.pallas_call(
+        hand_over,
+        out_shape=tuple(jax.ShapeDtypeStruct(r.shape, r.dtype) for r in results),
+        in_specs=[vmem] * 3,
+        out_specs=(vmem, vmem, vmem),
+    )(*results)
     return row_loss.reshape(rows), gi, gt
 
 

time: 82 us -> 76.5 us (0.933)
  local copies, waits for them, and re-layouts: 3.85 us -> 0 us
  Pallas kernels: 75.4 us -> 74.4 us
    unnamed x7 -> x0, local copies, waits for them, and re-layouts: 3.85 us -> none
    pallas_call x1, Pallas kernels: 75.4 us -> 72.3 us  [body(): pl.pallas_call(functools.partial(kernel, n, mp, pair), out_shape=(jax.Sha...]
    pallas_call x0 -> x1, Pallas kernels: none -> 2.09 us  [body(): pl.pallas_call(hand_over, out_shape=tuple((jax.ShapeDtypeStruct(r.shape,...]
where the time goes in v3:
time: 76.5 us; the launch traced here: 76.3 us
  Pallas kernels  74.4 us (97%)
  between operations  1.93 us (3%)
    pallas_call x1, Pallas kernels, body(): pl.pallas_call(functools.partial(kernel, n, mp, pair), out_shape=(jax.Sha...  72.3 us
    pallas_call x1, Pallas kernels, body(): pl.pallas_call(hand_over, out_shape=tuple((jax.ShapeDtypeStruct(r.shape,...  2.09 us

profile of v3, /device:TPU:0, one launch (start us, length us, event | category | flops | bytes accessed | tf_op | source)
XLA Modules:
  0.0 76.3 jit_solution(5559082207142802521)
XLA Ops:
  1.9 72.3 %shard_map.85 = (f32[1,256]{1,0:T(1,128)}, f32[288,288]{1,0:T(8,128)}, f32[288,288]{1,0:T(8,128)}) custom-call(f32[1]{0:T(128)S(6)} %copy.9.log_scale, f32[1]{0:T(128)S(6)} %copy.10.bias, bf16[256,1152]{1,0:T(8,128)(2,1)} %xi.1, bf16[256,1152]{1,0:T(8,128)(2,1)} %xt.1, bf16[288,1152]{1,0:T(8,128)(2,1)} %bitcast.3, bf16[288,1152]{1,0:T(8,128)(2,1)} %bitcast.4), custom_call_target="tpu_custom_call" | custom-call | tf_op jit(solution)/shard_map/pallas_call | solution.py:300
  74.2 2.1 %shard_map.86 = (f32[1,256]{1,0:T(1,128)}, f32[288,288]{1,0:T(8,128)}, f32[288,288]{1,0:T(8,128)}) custom-call(f32[1,256]{1,0:T(1,128)} %get-tuple-element.9.loss, f32[288,288]{1,0:T(8,128)} %get-tuple-element.10.gi, f32[288,288]{1,0:T(8,128)} %get-tuple-element.11.gt), custom_call_target="tpu_custom_call" | custom-call | tf_op jit(solution)/shard_map/pallas_call | solution.py:341

commit v4 on v3

--- a/solution.py
+++ b/solution.py
@@ -216,7 +216,7 @@
 
     def head_terms(which, back):
         copies = []
-        for k in peers:
+        for k in reversed(peers):
             term = dot_nn(turned[which, ahead(k)], back).astype(bf16)
             head_send[which, k, :padded] = term[:, :main]
             for low, top, left, right in groups(padded, padded):
@@ -224,6 +224,7 @@
             copies.append(to_dp(
                 head_send.at[which, k], head_recv.at[which, k], 2 + which, k, ahead(k)))
         sent.extend(copies)
+        copies.reverse()
         return dot_nn(turned[which, my_d], back), copies
 
     head_i, head_i_copies = head_terms(0, back_i)

time: 76.5 us -> 74.4 us (0.973)
  Pallas kernels: 74.4 us -> 72.1 us
    pallas_call x1, Pallas kernels: 72.3 us -> 70 us  [body(): pl.pallas_call(functools.partial(kernel, n, mp, pair), out_shape=(jax.Sha...]
where the time goes in v4:
time: 74.4 us; the launch traced here: 74.1 us
  Pallas kernels  72.1 us (97%)
  between operations  1.93 us (3%)
    pallas_call x1, Pallas kernels, body(): pl.pallas_call(functools.partial(kernel, n, mp, pair), out_shape=(jax.Sha...  70 us
    pallas_call x1, Pallas kernels, body(): pl.pallas_call(hand_over, out_shape=tuple((jax.ShapeDtypeStruct(r.shape,...  2.09 us

profile of v4, /device:TPU:0, one launch (start us, length us, event | category | flops | bytes accessed | tf_op | source)
XLA Modules:
  0.0 74.1 jit_solution(1819262148809316654)
XLA Ops:
  1.9 70.0 %shard_map.85 = (f32[1,256]{1,0:T(1,128)}, f32[288,288]{1,0:T(8,128)}, f32[288,288]{1,0:T(8,128)}) custom-call(f32[1]{0:T(128)S(6)} %copy.9.log_scale, f32[1]{0:T(128)S(6)} %copy.10.bias, bf16[256,1152]{1,0:T(8,128)(2,1)} %xi.1, bf16[256,1152]{1,0:T(8,128)(2,1)} %xt.1, bf16[288,1152]{1,0:T(8,128)(2,1)} %bitcast.3, bf16[288,1152]{1,0:T(8,128)(2,1)} %bitcast.4), custom_call_target="tpu_custom_call" | custom-call | tf_op jit(solution)/shard_map/pallas_call | solution.py:301
  72.0 2.1 %shard_map.86 = (f32[1,256]{1,0:T(1,128)}, f32[288,288]{1,0:T(8,128)}, f32[288,288]{1,0:T(8,128)}) custom-call(f32[1,256]{1,0:T(1,128)} %get-tuple-element.9.loss, f32[288,288]{1,0:T(8,128)} %get-tuple-element.10.gi, f32[288,288]{1,0:T(8,128)} %get-tuple-element.11.gt), custom_call_target="tpu_custom_call" | custom-call | tf_op jit(solution)/shard_map/pallas_call | solution.py:342

commit v5 on v4

--- a/solution.py
+++ b/solution.py
@@ -152,7 +152,8 @@
     for k, copy in zip(others, text_copies):
         copy.wait_recv()
         tall[0, :, k * width:(k + 1) * width] = pieces[k]
-    tall_copies = [to_dp(tall.at[0], tall.at[k], 0, k, ahead(k)) for k in peers]
+    tall_copies = [to_dp(tall.at[0], tall.at[k], 0, k, ahead(k)) for k in reversed(peers)]
+    tall_copies.reverse()
     wide_image[:, :width] = image[0]
     for which, x in enumerate((xi, xt)):
         across = x[...].T

time: 74.4 us -> 75.4 us (1.013); the launches traced: 74.1 us -> 73.9 us
  no operation moved by 1% of the time
where the time goes in v5:
time: 75.4 us; the launch traced here: 73.9 us
  Pallas kernels  72 us (95%)
  between operations  1.93 us (3%)
    pallas_call x1, Pallas kernels, body(): pl.pallas_call(functools.partial(kernel, n, mp, pair), out_shape=(jax.Sha...  69.9 us
    pallas_call x1, Pallas kernels, body(): pl.pallas_call(hand_over, out_shape=tuple((jax.ShapeDtypeStruct(r.shape,...  2.09 us

profile of v5, /device:TPU:0, one launch (start us, length us, event | category | flops | bytes accessed | tf_op | source)
XLA Modules:
  0.0 73.9 jit_solution(3591573367552421888)
XLA Ops:
  1.9 69.9 %shard_map.85 = (f32[1,256]{1,0:T(1,128)}, f32[288,288]{1,0:T(8,128)}, f32[288,288]{1,0:T(8,128)}) custom-call(f32[1]{0:T(128)S(6)} %copy.9.log_scale, f32[1]{0:T(128)S(6)} %copy.10.bias, bf16[256,1152]{1,0:T(8,128)(2,1)} %xi.1, bf16[256,1152]{1,0:T(8,128)(2,1)} %xt.1, bf16[288,1152]{1,0:T(8,128)(2,1)} %bitcast.3, bf16[288,1152]{1,0:T(8,128)(2,1)} %bitcast.4), custom_call_target="tpu_custom_call" | custom-call | tf_op jit(solution)/shard_map/pallas_call | solution.py:302
  71.8 2.1 %shard_map.86 = (f32[1,256]{1,0:T(1,128)}, f32[288,288]{1,0:T(8,128)}, f32[288,288]{1,0:T(8,128)}) custom-call(f32[1,256]{1,0:T(1,128)} %get-tuple-element.9.loss, f32[288,288]{1,0:T(8,128)} %get-tuple-element.10.gi, f32[288,288]{1,0:T(8,128)} %get-tuple-element.11.gt), custom_call_target="tpu_custom_call" | custom-call | tf_op jit(solution)/shard_map/pallas_call | solution.py:343
